TPU v7x, 512 devices: a whole 4x8x8 slice. The times are simulated.
512 devices in a mesh: dp: 32 (over z, y_lo), ctx: 16 (over x, y_hi, core).
Axes of the slice: x: 4, y: 8 (y_hi: 2, y_lo: 4; y = y_hi * 4 + y_lo), z: 8, core: 2. Of those that a mesh axis runs over, the one named last changes fastest.
Arguments:
- frame_input: bfloat16 [64, 1024, 1536], P('dp', 'ctx'), may hold values from -6 to 6
- queries: bfloat16 [64, 1024, 768], P('dp', 'ctx'), may hold values from -18 to 18
- key_proj: bfloat16 [64, 1024, 768], P('dp', 'ctx'), may hold values from -18 to 18
- value_proj: bfloat16 [64, 1024, 768], P('dp', 'ctx'), may hold values from -6 to 6
- out_weight: bfloat16 [1536, 768], P('ctx', 'dp'), may hold values from -0.21875 to 0.21875
- conv_weight: bfloat16 [31, 1536], P(None, 'dp'), may hold values from -1 to 1
- lengths: int32 [64], P('dp'), may hold values from 256 to 1024, as said below
- grad_output: bfloat16 [64, 1024, 1536], P('dp', 'ctx'), may hold values from -6 to 6
Outputs:
- block_output: bfloat16 [64, 1024, 1536], P('dp', 'ctx')
- grad_input: bfloat16 [64, 1024, 1536], P('dp', 'ctx')
- grad_queries: bfloat16 [64, 1024, 768], P('dp', 'ctx')
- grad_keys: bfloat16 [64, 1024, 768], P('dp', 'ctx')
- grad_values: bfloat16 [64, 1024, 768], P('dp', 'ctx')
- grad_out_weight: float32 [1536, 768], P('ctx', 'dp')
- grad_conv_weight: float32 [31, 1536], P(None, 'dp')
Inputs may be any that keep to these rules, and one draw needn't show every extreme that they name: `lengths`: at least one utterance of every draw fills all 1024 frame slots.
All inputs are finite; a program needn't handle non-finite values.
Results may differ from a plain program's by a relative error of at most 0.035.
Values may be sent and summed in bfloat16 or wider, within the bound.
A program may use at most 128 MiB of HBM per device.

v0:
```python
import jax
import jax.numpy as jnp
from jax import lax
from jax.sharding import PartitionSpec as P

HEAD_DIM = 64
masked_score = -1e30


def padded_2(array, sides, width):
    for axis, dim in sides:
        size, length = (lax.axis_size(axis), array.shape[dim])
        up = [(i, (i + 1) % size) for i in range(size - 1)]
        down = [(j, i) for i, j in up]
        last = lax.slice_in_dim(array, length - width, length, axis=dim)
        leading = lax.slice_in_dim(array, 0, width, axis=dim)
        before = lax.ppermute(last, axis, up)
        after = lax.ppermute(leading, axis, down)
        array = jnp.concatenate([before, array, after], axis=dim)
    return array


def depthwise(lhs, rhs):
    return lax.conv_general_dilated(
        lhs,
        rhs,
        (1,),
        "VALID",
        dimension_numbers=("NWC", "WIO", "NWC"),
        feature_group_count=lhs.shape[2],
        precision=lax.Precision.HIGHEST,
    )


def per_device(
    frame_input, queries, key_proj, value_proj, out_weight, conv_weight, lengths, grad_output
):
    utt_count = frame_input.shape[0]
    frame_count = frame_input.shape[1]
    inner_width = queries.shape[2]
    head_count = inner_width // HEAD_DIM
    group_heads = max((g for g in range(1, 7) if head_count % g == 0))
    group_count = head_count // group_heads
    group_width = group_heads * HEAD_DIM
    tap_count = conv_weight.shape[0]
    half_span = (tap_count - 1) // 2
    score_scale = HEAD_DIM ** (-0.5)
    total_frames = frame_count * lax.axis_size("ctx")
    offset = lax.axis_index("ctx") * frame_count
    own_valid = (offset + jnp.arange(frame_count, dtype=jnp.int32))[None, :] < lengths[:, None]
    all_valid = jnp.arange(total_frames, dtype=jnp.int32)[None, :] < lengths[:, None]

    def grouped(values):
        row_count = values.shape[1]
        return values.reshape(utt_count, row_count, group_count, group_width).transpose(2, 0, 1, 3)

    def ungrouped(values):
        row_count = values.shape[2]
        return values.transpose(1, 2, 0, 3).reshape(utt_count, row_count, group_count * group_width)

    def split_heads(values):
        return values.reshape(utt_count, values.shape[1], group_heads, HEAD_DIM)

    def stats_grouped(values):
        row_count = values.shape[1]
        return values.reshape(utt_count, row_count, group_count, group_heads).transpose(2, 0, 3, 1)

    def masked_scores(query_block, key_block, key_mask):
        scores = (
            jnp.einsum(
                "uqgd,ukgd->ugqk", query_block, key_block, preferred_element_type=jnp.float32
            )
            * score_scale
        )
        return jnp.where(key_mask[:, None, None, :], scores, masked_score)

    taps = lax.all_gather(conv_weight, "dp", axis=1, tiled=True).astype(jnp.float32)
    panel_rows = lax.all_gather(out_weight, "dp", axis=1, tiled=True)
    weight_full = lax.all_gather(panel_rows, "ctx", axis=0, tiled=True)
    all_keys, all_values = (
        lax.all_gather(key_proj, "ctx", axis=1, tiled=True),
        lax.all_gather(value_proj, "ctx", axis=1, tiled=True),
    )
    query_groups = grouped(queries)
    key_groups = grouped(all_keys)
    value_groups = grouped(all_values)

    def forward_group(unused, items):
        query_group, key_group, value_group = items
        query_block = split_heads(query_group)
        scores = masked_scores(query_block, split_heads(key_group), all_valid)
        largest = jnp.max(scores, axis=-1)
        log_group = largest + jnp.log(jnp.sum(jnp.exp(scores - largest[..., None]), axis=-1))
        weights_low = jnp.exp(scores - log_group[..., None]).astype(jnp.bfloat16)
        attended_group = jnp.einsum(
            "ugqk,ukgd->uqgd",
            weights_low,
            split_heads(value_group),
            preferred_element_type=jnp.float32,
        )
        return (None, (log_group, attended_group.reshape(utt_count, frame_count, group_width)))

    _, (log_groups, attended_groups) = lax.scan(
        forward_group, None, (query_groups, key_groups, value_groups)
    )
    attended = ungrouped(attended_groups).astype(jnp.bfloat16)
    log_total = log_groups.transpose(1, 3, 0, 2).reshape(utt_count, frame_count, head_count)
    projected = jnp.einsum("ufe,de->ufd", attended, weight_full, preferred_element_type=jnp.float32)
    hidden = (frame_input.astype(jnp.float32) + projected).astype(jnp.bfloat16)
    masked_hidden = jnp.where(own_valid[:, :, None], hidden, jnp.zeros_like(hidden))
    padded = padded_2(masked_hidden, (("ctx", 1),), half_span).astype(jnp.float32)
    conv_sum = depthwise(padded, taps[:, None, :])
    sigmoid = jax.nn.sigmoid(conv_sum)
    block_output = (hidden.astype(jnp.float32) + conv_sum * sigmoid).astype(jnp.bfloat16)
    grad_local = grad_output.astype(jnp.float32)
    swish_slope = sigmoid * (1.0 + conv_sum * (1.0 - sigmoid))
    grad_conv = (grad_local * swish_slope).astype(jnp.bfloat16)
    grad_padded = padded_2(grad_conv, (("ctx", 1),), half_span).astype(jnp.float32)
    back_sum = depthwise(grad_padded, taps[::-1][:, None, :])
    grad_hidden = (grad_local + jnp.where(own_valid[:, :, None], back_sum, 0.0)).astype(
        jnp.bfloat16
    )
    grad_conv_wide = grad_conv.astype(jnp.float32)
    kernel_term = jnp.zeros((tap_count, conv_sum.shape[2]), jnp.float32)
    for utt_index in range(utt_count):
        kernel_term = (
            kernel_term
            + depthwise(padded[utt_index : utt_index + 1], grad_conv_wide[utt_index][:, None, :])[0]
        )
    kernel_whole = lax.psum(kernel_term.astype(jnp.bfloat16), "ctx")
    grad_conv_weight = lax.psum_scatter(kernel_whole, "dp", scatter_dimension=1, tiled=True).astype(
        jnp.float32
    )
    grad_attended = jnp.einsum(
        "ufd,de->ufe", grad_hidden, weight_full, preferred_element_type=jnp.float32
    ).astype(jnp.bfloat16)
    row_delta = jnp.sum(
        grad_attended.astype(jnp.float32).reshape(utt_count, frame_count, head_count, HEAD_DIM)
        * attended.astype(jnp.float32).reshape(utt_count, frame_count, head_count, HEAD_DIM),
        axis=-1,
    )
    grad_groups = grouped(grad_attended)

    def query_group_step(unused, items):
        query_group, key_group, value_group, grad_group, log_group, delta_group = items
        key_block = split_heads(key_group)
        weights = jnp.exp(
            masked_scores(split_heads(query_group), key_block, all_valid) - log_group[..., None]
        )
        grad_weights = jnp.einsum(
            "uqgd,ukgd->ugqk",
            split_heads(grad_group),
            split_heads(value_group),
            preferred_element_type=jnp.float32,
        )
        grad_scores = (weights * (grad_weights - delta_group[..., None])).astype(jnp.bfloat16)
        query_sum = jnp.einsum(
            "ugqk,ukgd->uqgd", grad_scores, key_block, preferred_element_type=jnp.float32
        )
        return (None, query_sum.reshape(utt_count, frame_count, group_width))

    _, query_sums = lax.scan(
        query_group_step,
        None,
        (
            query_groups,
            key_groups,
            value_groups,
            grad_groups,
            stats_grouped(log_total),
            stats_grouped(row_delta),
        ),
    )
    grad_queries = (ungrouped(query_sums) * score_scale).astype(jnp.bfloat16)
    total_log, total_delta = (
        lax.all_gather(log_total, "ctx", axis=1, tiled=True),
        lax.all_gather(row_delta, "ctx", axis=1, tiled=True),
    )
    own_key_groups = grouped(key_proj)
    own_value_groups = grouped(value_proj)
    group_zeros = jnp.zeros((group_count, utt_count, frame_count, group_width), jnp.float32)
    start_sums = (group_zeros, group_zeros)
    query_all, grad_all = (
        lax.all_gather(queries, "ctx", axis=1, tiled=True),
        lax.all_gather(grad_attended, "ctx", axis=1, tiled=True),
    )
    log_piece = stats_grouped(total_log)
    delta_piece = stats_grouped(total_delta)

    def key_group_step(unused, items):
        (
            query_group,
            grad_group,
            log_group,
            delta_group,
            key_group,
            value_group,
            key_sum,
            value_sum,
        ) = items
        query_block = split_heads(query_group)
        grad_block = split_heads(grad_group)
        weights = jnp.exp(
            masked_scores(query_block, split_heads(key_group), own_valid) - log_group[..., None]
        )
        grad_weights = jnp.einsum(
            "uqgd,ukgd->ugqk",
            grad_block,
            split_heads(value_group),
            preferred_element_type=jnp.float32,
        )
        grad_scores = (weights * (grad_weights - delta_group[..., None])).astype(jnp.bfloat16)
        key_next = key_sum + jnp.einsum(
            "ugqk,uqgd->ukgd", grad_scores, query_block, preferred_element_type=jnp.float32
        ).reshape(utt_count, frame_count, group_width)
        value_next = value_sum + jnp.einsum(
            "ugqk,uqgd->ukgd",
            weights.astype(jnp.bfloat16),
            grad_block,
            preferred_element_type=jnp.float32,
        ).reshape(utt_count, frame_count, group_width)
        return (None, (key_next, value_next))

    _, result_sums = lax.scan(
        key_group_step,
        None,
        (
            grouped(query_all),
            grouped(grad_all),
            log_piece,
            delta_piece,
            own_key_groups,
            own_value_groups,
            start_sums[0],
            start_sums[1],
        ),
    )
    key_sum, value_sum = result_sums
    grad_keys = (ungrouped(key_sum) * score_scale).astype(jnp.bfloat16)
    grad_values = ungrouped(value_sum).astype(jnp.bfloat16)
    hidden_cols = lax.slice_in_dim(
        grad_hidden, 0, weight_full.shape[0] // lax.axis_size("ctx") * lax.axis_size("ctx"), axis=2
    )
    panel_share = lax.psum_scatter(
        jnp.einsum("ufd,ufe->de", hidden_cols, attended, preferred_element_type=jnp.float32).astype(
            jnp.bfloat16
        ),
        "ctx",
        scatter_dimension=0,
        tiled=True,
    )
    grad_out_weight = lax.psum_scatter(panel_share, "dp", scatter_dimension=1, tiled=True).astype(
        jnp.float32
    )
    return (
        block_output,
        grad_hidden,
        grad_queries,
        grad_keys,
        grad_values,
        grad_out_weight,
        grad_conv_weight,
    )


def solution(mesh):
    placed = (
        P("dp", "ctx", None),
        P("dp", "ctx", None),
        P("dp", "ctx", None),
        P("dp", "ctx", None),
        P("ctx", "dp"),
        P(None, "dp"),
        P("dp"),
        P("dp", "ctx", None),
    )
    return jax.shard_map(
        per_device,
        mesh=mesh,
        in_specs=placed,
        out_specs=(
            P("dp", "ctx", None),
            P("dp", "ctx", None),
            P("dp", "ctx", None),
            P("dp", "ctx", None),
            P("dp", "ctx", None),
            P("ctx", "dp"),
            P(None, "dp"),
        ),
        check_vma=False,
    )
```

profile of v0, /device:TPU:1, one launch (start us, length us, event | category | flops | bytes accessed | tf_op | source)
XLA Modules:
  0.0 1105.4 jit_solution(739384458572072141)
XLA Ops:
  7.2 1.8 copy.131
  11.0 77.3 %all_gather.29 = bf16[96,768]{0,1:T(8,128)(2,1)S(1)} all-gather(bf16[96,24]{0,1:T(8,128)(2,1)} %param.18), channel_id=1, replica_groups=mesh['dp'=32,'ctx'=16] {'dp'}, dimensions={1}, use_global_device_ids=true | all-gather | bytes 152064 | tf_op jit(solution)/shard_map/all_gather | solution.py:78
  92.1 2.1 all-gather.7.cloned.1.call-done
  94.3 7.0 copy.132
  101.3 2.0 copy.136
  103.3 64.5 %all-gather.9.cloned.1.call-done = bf16[2,1024,768]{2,0,1:T(2,128)(2,1)} async-done(((bf16[2,64,768]{2,0,1:T(2,128)(2,1)}), bf16[2,1024,768]{2,0,1:T(2,128)(2,1)}) %all-gather.9.cloned.1.call-update) | async-done | bytes 3145744 | tf_op jit(solution)/shard_map/all_gather | solution.py:82
  167.8 7.0 copy.134
  174.8 2.0 copy.137
  176.9 16.0 %while.37 = (s32[]{:T(128)}, f32[2,2,6,64]{3,2,1,0:T(8,128)}, bf16[2,2,64,384]{3,2,0,1:T(8,128)(2,1)}, bf16[2,2,64,384]{3,2,1,0:T(8,128)(2,1)}, bf16[2,2,1024,38...) while((s32[]{:T(128)}, f32[2,2,6,64]{3,2,1,0:T(8,128)}, ...), condition=%wide.region_3.4_spmd.clone, body=%wide.region_0.3_spmd.clone.sunk | while | flops 209978624 | bytes 21468332 | solution.py:103
  177.6 2.2 constant_dynamic-slice_fusion.23
  185.6 2.2 constant_dynamic-slice_fusion.23
  193.8 43.9 %all-gather.11.cloned.1.call-done = bf16[1536,768]{1,0:T(8,128)(2,1)} async-done(((bf16[96,768]{1,0:T(8,128)(2,1)}), bf16[1536,768]{1,0:T(8,128)(2,1)}) %all-gather.11.cloned.1.call-update) | async-done | bytes 2359312 | tf_op jit(solution)/shard_map/all_gather | solution.py:79
  237.7 2.6 broadcast_select_fusion
  240.3 2.2 collective-permute-start.1
  242.5 7.3 collective-permute-start
  249.8 64.3 %all-gather = bf16[32,48,31]{1,2,0:T(8,128)(2,1)S(1)} all-gather(bf16[1,48,31]{1,2,0:T(8,128)(2,1)S(1)} %bitcast.212), channel_id=1, replica_groups=mesh['dp'=32,'ctx'=16] {'dp'}, dimensions={0}, use_global_device_ids=true | all-gather | bytes 98208 | tf_op jit(solution)/shard_map/all_gather | solution.py:77
  314.8 2.7 fusion.54
  318.6 11.0 collective-permute-start.3
  329.6 6.8 collective-permute-start.2
  338.3 2.3 fusion.52
  340.9 2.2 bitcast_convert_fusion
  344.2 1.9 fusion.49
  346.1 1.9 fusion.43
  349.2 90.0 %reduce-scatter.6.cloned.1.call-done = bf16[96,768]{1,0:T(8,128)(2,1)} async-done(((bf16[1536,768]{1,0:T(8,128)(2,1)}), bf16[96,768]{1,0:T(8,128)(2,1)}) %reduce-scatter.6.cloned.1.call-update) | async-done | bytes 147472 | tf_op jit(solution)/shard_map/reduce_scatter | solution.py:244
  446.6 42.3 %all_gather.33 = f32[2,1024,12]{2,0,1:T(2,128)S(1)} all-gather(f32[2,64,12]{2,0,1:T(2,128)S(1)} %copy.161), channel_id=1, replica_groups=mesh['dp'=32,'ctx'=16] {'ctx'}, dimensions={1}, use_global_device_ids=true | all-gather | bytes 104448 | tf_op jit(solution)/shard_map/all_gather | solution.py:176
  490.0 29.2 %all-gather.13.cloned.1.call-done = bf16[2,1024,768]{2,0,1:T(2,128)(2,1)} async-done(((bf16[2,64,768]{2,0,1:T(2,128)(2,1)}), bf16[2,1024,768]{2,0,1:T(2,128)(2,1)}) %all-gather.13.cloned.1.call-update) | async-done | bytes 3145744 | tf_op jit(solution)/shard_map/all_gather | solution.py:184
  519.1 8.7 copy.159
  531.5 29.7 %while.38 = (s32[]{:T(128)}, f32[2,2,64,384]{2,3,1,0:T(8,128)}, bf16[2,2,1024,384]{2,3,1,0:T(8,128)(2,1)}, bf16[2,2,64,384]{3,2,1,0:T(8,128)(2,1)}, f32[2,2,6,64...) while((s32[]{:T(128)}, f32[2,2,64,384]{2,3,1,0:T(8,128)}, ...), condition=%wide.region_6.7_spmd.clone, body=%wide.region_5.6_spmd.clone.sunk | while | flops 306710528 | bytes 19099784 | solution.py:162
  531.5 2.2 constant_dynamic-slice_fusion.25
  536.4 2.2 fusion.108
  542.2 3.4 fusion.109
  546.3 2.2 constant_dynamic-slice_fusion.25
  551.2 2.2 fusion.108
  557.0 3.4 fusion.109
  563.4 37.6 %all_gather.35 = f32[2,1024,12]{2,0,1:T(2,128)S(1)} all-gather(f32[2,64,12]{2,0,1:T(2,128)} %copy.164), channel_id=1, replica_groups=mesh['dp'=32,'ctx'=16] {'ctx'}, dimensions={1}, use_global_device_ids=true | all-gather | bytes 104448 | tf_op jit(solution)/shard_map/all_gather | solution.py:177
  601.5 59.2 %reduce-scatter.8.cloned.1.call-done = bf16[48,31]{1,0:T(8,128)(2,1)} async-done(((bf16[1536,31]{1,0:T(8,128)(2,1)}), bf16[48,31]{1,0:T(8,128)(2,1)}) %reduce-scatter.8.cloned.1.call-update) | async-done | bytes 2992
  661.6 68.0 %psum.8 = bf16[31,48]{1,0:T(8,128)(2,1)S(1)} all-reduce(bf16[31,48]{1,0:T(8,128)(2,1)S(1)} %copy.181), channel_id=1, replica_groups=mesh['dp'=32,'ctx'=16] {'ctx'}, use_global_device_ids=true, to_apply=%region_11.12 | all-reduce | flops 1488 | bytes 5952 | tf_op jit(solution)/shard_map/psum | solution.py:130
  730.2 222.8 %all-reduce.3.cloned.1.call-done = bf16[96,768]{1,0:T(8,128)(2,1)} async-done(((bf16[96,768]{1,0:T(8,128)(2,1)}), bf16[96,768]{1,0:T(8,128)(2,1)}) %all-reduce.3.cloned.1.call-update) | async-done | bytes 147472
  954.5 91.6 %all-gather.15.cloned.1.call-done = bf16[2,1024,768]{2,1,0:T(8,128)(2,1)} async-done(((bf16[2,64,768]{2,1,0:T(8,128)(2,1)}), bf16[2,1024,768]{2,1,0:T(8,128)(2,1)}) %all-gather.15.cloned.1.call-update) | async-done | bytes 3145744 | tf_op jit(solution)/shard_map/all_gather | solution.py:185
  1046.1 5.8 reshape.203
  1051.9 6.9 copy.163
  1059.8 34.6 %while.39 = (s32[]{:T(128)}, f32[2,2,64,384]{2,3,1,0:T(8,128)}, bf16[2,2,64,384]{2,3,1,0:T(8,128)(2,1)}, bf16[2,2,1024,384]{2,3,0,1:T(8,128)(2,1)}, bf16[2,2,64,...) while((s32[]{:T(128)}, f32[2,2,64,384]{2,3,1,0:T(8,128)}, ...), condition=%wide.region_8.9_spmd.clone, body=%wide.region_7.8_spmd.clone.sunk | while | flops 410517632 | bytes 39764904 | solution.py:224
  1062.5 2.3 fusion.117
  1069.1 3.3 fusion.118
  1073.2 3.0 fusion.119
  1079.8 2.3 fusion.117
  1086.4 3.3 fusion.118
  1090.5 3.0 fusion.119
  (180 shorter events, 77.7 us)
Async XLA Ops:
  7.2 87.1 %all-gather.7.cloned.1.call-start = ((), (), s32[]{:S(2)}) async-start(), calls=%async_computation.2 | async-start | bytes 3342336 | tf_op jit(solution)/shard_map/all_gather | solution.py:81
  9.0 158.8 %all-gather.9.cloned.1.call-start = ((), (), s32[]{:S(2)}) async-start(), calls=%async_computation.3 | async-start | bytes 3342336 | tf_op jit(solution)/shard_map/all_gather | solution.py:82
  10.9 226.8 %all-gather.11.cloned.1.call-start = ((), (), s32[]{:S(2)}) async-start(), calls=%async_computation.4 | async-start | bytes 2506752 | tf_op jit(solution)/shard_map/all_gather | solution.py:79
  89.1 350.1 %reduce-scatter.6.cloned.1.call-start = ((), (), s32[]{:S(2)}) async-start(), calls=%async_computation.7 | async-start | bytes 2506752 | tf_op jit(solution)/shard_map/reduce_scatter | solution.py:244
  90.8 0.6 copy-start.16
  182.9 1.2 copy-start.12
  184.2 0.7 copy-start.13
  190.9 1.2 copy-start.12
  192.2 0.7 copy-start.13
  192.9 57.0 %copy-start.15 = (bf16[31,48]{1,0:T(8,128)(2,1)S(1)}, bf16[31,48]{1,0:T(8,128)(2,1)}, u32[]{:S(2)}) copy-start(bf16[31,48]{1,0:T(8,128)(2,1)} %param.19) | copy-start | bytes 8932
  240.3 74.3 %collective-permute-start.1 = (bf16[2,15,1536]{2,1,0:T(8,128)(2,1)S(1)}, bf16[2,15,1536]{2,1,0:T(8,128)(2,1)S(1)}, u32[]{:S(2)}, u32[]{:S(2)}) collective-permute-start(bf16[2,15,1536]{2,1,0:T(8,128)(2,1)S(1)} %get-tuple-element.409), channel_id=1, source_target_pairs={{1,0},{2,1},{3,2},{4,3},{5,4},{6,5},{7,6},{8,7},{9,8},{10,9},{11,1... | collective-permute-start | bytes 276488 | tf_op jit(solution)/shard_map/ppermute | solution.py:18
  242.5 72.1 %collective-permute-start = (bf16[2,15,1536]{2,1,0:T(8,128)(2,1)S(1)}, bf16[2,15,1536]{2,1,0:T(8,128)(2,1)S(1)}, u32[]{:S(2)}, u32[]{:S(2)}) collective-permute-start(bf16[2,15,1536]{2,1,0:T(8,128)(2,1)S(1)} %get-tuple-element.408), channel_id=1, source_target_pairs={{0,1},{1,2},{2,3},{3,4},{4,5},{5,6},{6,7},{7,8},{8,9},{9,10},{10,1... | collective-permute-start | bytes 276488 | tf_op jit(solution)/shard_map/ppermute | solution.py:17
  314.8 2.7 copy-start.4
  318.6 18.2 %collective-permute-start.3 = (bf16[2,15,1536]{2,1,0:T(8,128)(2,1)S(1)}, bf16[2,15,1536]{2,1,0:T(8,128)(2,1)S(1)}, u32[]{:S(2)}, u32[]{:S(2)}) collective-permute-start(bf16[2,15,1536]{2,1,0:T(8,128)(2,1)S(1)} %get-tuple-element.407), channel_id=1, source_target_pairs={{1,0},{2,1},{3,2},{4,3},{5,4},{6,5},{7,6},{8,7},{9,8},{10,9},{11,1... | collective-permute-start | bytes 276488 | tf_op jit(solution)/shard_map/ppermute | solution.py:18
  329.6 8.5 collective-permute-start.2
  340.6 2.6 copy-start.9
  340.9 98.6 %copy-start.2 = (bf16[2,64,1536]{2,1,0:T(8,128)(2,1)}, bf16[2,64,1536]{2,1,0:T(8,128)(2,1)S(1)}, u32[]{:S(2)}) copy-start(bf16[2,64,1536]{2,1,0:T(8,128)(2,1)S(1)} %fusion.48) | copy-start | bytes 1179652
  343.1 176.0 %all-gather.13.cloned.1.call-start = ((), (), s32[]{:S(2)}) async-start(), calls=%async_computation.5 | async-start | bytes 3342336 | tf_op jit(solution)/shard_map/all_gather | solution.py:184
  344.1 316.7 %reduce-scatter.8.cloned.1.call-start = ((), (), s32[]{:S(2)}) async-start(), calls=%async_computation.8 | async-start | bytes 405504
  346.1 93.4 %copy-start.1 = (bf16[1536,768]{1,0:T(8,128)(2,1)S(1)}, bf16[1536,768]{1,0:T(8,128)(2,1)}, u32[]{:S(2)}) copy-start(bf16[1536,768]{1,0:T(8,128)(2,1)} %all-gather.11.cloned.1.call-done) | copy-start | bytes 7077892
  348.1 92.6 %copy-start.10 = (bf16[2,64,768]{2,1,0:T(8,128)(2,1)S(1)}, bf16[2,64,768]{2,1,0:T(8,128)(2,1)}, u32[]{:S(2)}) copy-start(bf16[2,64,768]{2,1,0:T(8,128)(2,1)} %param.16) | copy-start | bytes 589828
  348.1 92.6 %copy-start.11 = (bf16[2,64,768]{2,1,0:T(8,128)(2,1)S(1)}, bf16[2,64,768]{2,1,0:T(8,128)(2,1)}, u32[]{:S(2)}) copy-start(bf16[2,64,768]{2,1,0:T(8,128)(2,1)} %param.17) | copy-start | bytes 589828
  348.1 96.8 %copy-start.14 = (bf16[2,2,64,384]{3,2,0,1:T(8,128)(2,1)S(1)}, bf16[2,2,64,384]{3,2,0,1:T(8,128)(2,1)}, u32[]{:S(2)}) copy-start(bf16[2,2,64,384]{3,2,0,1:T(8,128)(2,1)} %get-tuple-element.145) | copy-start | bytes 589828
  349.1 603.8 %all-reduce.3.cloned.1.call-start = ((), (), s32[]{:S(2)}) async-start(), calls=%async_computation.9 | async-start | bytes 294912
  439.2 606.9 %all-gather.15.cloned.1.call-start = ((), (), s32[]{:S(2)}) async-start(), calls=%async_computation.6 | async-start | bytes 3342336 | tf_op jit(solution)/shard_map/all_gather | solution.py:185
  490.0 37.9 %copy-start.3 = (bf16[2,64,768]{2,1,0:T(8,128)(2,1)S(1)}, bf16[2,64,768]{2,1,0:T(8,128)(2,1)}, u32[]{:S(2)}) copy-start(bf16[2,64,768]{2,1,0:T(8,128)(2,1)} %fusion.44) | copy-start | bytes 589828
  1051.9 7.8 copy-start.17
  1059.8 5.6 copy-start.7
  1062.5 2.8 copy-start
  1073.2 3.0 copy-start.5
  1073.2 3.8 copy-start.8
  1076.3 0.7 copy-start.6
  1077.1 5.6 copy-start.7
  1079.8 2.8 copy-start
  1090.5 3.0 copy-start.5
  1090.5 3.8 copy-start.8
  1093.6 0.7 copy-start.6
Sparse Core Ops, SparseCore 0:
  11.8 82.3 all-gather.6
  98.1 69.6 all-gather.8
  171.7 65.9 all-gather.10
  343.3 95.8 reduce-scatter.5
  442.9 76.1 all-gather.12
  521.8 138.9 reduce-scatter.7
  663.9 288.9 all-reduce.2
  956.3 89.7 all-gather.14
where the time goes:
time: 1110 us
  waiting for transfers between devices  605 us (55%)
  blocking collectives  290 us (26%)
  local copies, waits for them, and re-layouts  105 us (9%)
  matrix products  46.7 us (4%)
  starting transfers between devices  27.7 us (2%)
  other arithmetic  15.8 us (1%)
  between operations  15.2 us (1%)
    unnamed x10, waiting for transfers between devices  282 us
    all_gather x1, waiting for transfers between devices, per_device(): lax.all_gather(grad_attended, 'ctx', axis=1, tiled=True)  91.6 us
    reduce_scatter x1, waiting for transfers between devices, per_device(): lax.psum_scatter(jnp.einsum('ufd,ufe->de', hidden_cols, attended, preferr...  90 us
    all_gather x1, blocking collectives, per_device(): panel_rows = lax.all_gather(out_weight, 'dp', axis=1, tiled=True)  77.3 us
    psum x1, blocking collectives, per_device(): kernel_whole = lax.psum(kernel_term.astype(jnp.bfloat16), 'ctx')  68 us
    all_gather x1, waiting for transfers between devices, per_device(): lax.all_gather(value_proj, 'ctx', axis=1, tiled=True)  64.5 us
    all_gather x1, blocking collectives, per_device(): lax.all_gather(conv_weight, 'dp', axis=1, tiled=True).astype(jnp.float32)  64.3 us
    all_gather x1, waiting for transfers between devices, per_device(): weight_full = lax.all_gather(panel_rows, 'ctx', axis=0, tiled=True)  43.9 us
  transfers between devices with their start and end apart: 12, of which 9 were waited for; matrix products, arithmetic and copies ran while one was open for 9% of the time, Pallas kernels for 0%

commit v1 on v0

--- a/solution.py
+++ b/solution.py
@@ -1,3 +1,4 @@
+import functools
 import jax
 import jax.numpy as jnp
 from jax import lax
@@ -5,6 +6,13 @@
 
 HEAD_DIM = 64
 masked_score = -1e30
+
+
+def scan_panel_by_axis(array_here, row_axis):
+    return jnp.sum(lax.all_gather(array_here, axis_name=row_axis), axis=0)
+
+
+edit_the_shapes = functools.partial(scan_panel_by_axis, row_axis="ctx")
 
 
 def padded_2(array, sides, width):
@@ -127,7 +135,7 @@
             kernel_term
             + depthwise(padded[utt_index : utt_index + 1], grad_conv_wide[utt_index][:, None, :])[0]
         )
-    kernel_whole = lax.psum(kernel_term.astype(jnp.bfloat16), "ctx")
+    kernel_whole = edit_the_shapes(kernel_term.astype(jnp.bfloat16))
     grad_conv_weight = lax.psum_scatter(kernel_whole, "dp", scatter_dimension=1, tiled=True).astype(
         jnp.float32
     )

time: 1110 us -> 1160 us (1.045)
  waiting for transfers between devices: 605 us -> 719 us
  blocking collectives: 290 us -> 224 us
    psum x1 -> x0, blocking collectives: 68 us -> none  [per_device(): kernel_whole = lax.psum(kernel_term.astype(jnp.bfloat16), 'ctx')]
    unnamed x10 -> x11, waiting for transfers between devices: 282 us -> 346 us
    all_gather x0 -> x1, waiting for transfers between devices: none -> 45.4 us  [scan_panel_by_axis(): return jnp.sum(lax.all_gather(array_here, axis_name=row_axis), axis=0)]
  transfers between devices with their start and end apart: 12 -> 13, of which waited for: 9 -> 10; matrix products, arithmetic and copies ran while one was open for 9% -> 9% of each run, Pallas kernels for 0% -> 0%
where the time goes in v1:
time: 1160 us
  waiting for transfers between devices  719 us (62%)
  blocking collectives  224 us (19%)
  local copies, waits for them, and re-layouts  106 us (9%)
  matrix products  46.6 us (4%)
  starting transfers between devices  27.8 us (2%)
  other arithmetic  17.5 us (2%)
  between operations  14.9 us (1%)
    unnamed x11, waiting for transfers between devices  346 us
    reduce_scatter x1, waiting for transfers between devices, per_device(): lax.psum_scatter(jnp.einsum('ufd,ufe->de', hidden_cols, attended, preferr...  95 us
    all_gather x1, waiting for transfers between devices, per_device(): lax.all_gather(grad_attended, 'ctx', axis=1, tiled=True)  91.6 us
    all_gather x1, blocking collectives, per_device(): panel_rows = lax.all_gather(out_weight, 'dp', axis=1, tiled=True)  77.3 us
    all_gather x1, waiting for transfers between devices, per_device(): lax.all_gather(value_proj, 'ctx', axis=1, tiled=True)  64.6 us
    all_gather x1, blocking collectives, per_device(): lax.all_gather(conv_weight, 'dp', axis=1, tiled=True).astype(jnp.float32)  64.3 us
    all_gather x1, waiting for transfers between devices, scan_panel_by_axis(): return jnp.sum(lax.all_gather(array_here, axis_name=row_axis), axis=0)  45.4 us
    all_gather x1, waiting for transfers between devices, per_device(): weight_full = lax.all_gather(panel_rows, 'ctx', axis=0, tiled=True)  43.9 us
  transfers between devices with their start and end apart: 13, of which 10 were waited for; matrix products, arithmetic and copies ran while one was open for 9% of the time, Pallas kernels for 0%

profile of v1, /device:TPU:1, one launch (start us, length us, event | category | flops | bytes accessed | tf_op | source)
XLA Modules:
  0.0 1156.0 jit_solution(6337697547938895316)
XLA Ops:
  7.2 1.8 copy.132
  11.0 77.3 %all_gather.33 = bf16[96,768]{0,1:T(8,128)(2,1)S(1)} all-gather(bf16[96,24]{0,1:T(8,128)(2,1)} %param.18), channel_id=1, replica_groups=mesh['dp'=32,'ctx'=16] {'dp'}, dimensions={1}, use_global_device_ids=true | all-gather | bytes 152064 | tf_op jit(solution)/shard_map/all_gather | solution.py:86
  92.1 2.2 all-gather.8.cloned.1.call-done
  94.3 7.0 copy.133
  101.3 2.0 copy.137
  103.3 64.6 %all-gather.10.cloned.1.call-done = bf16[2,1024,768]{2,0,1:T(2,128)(2,1)} async-done(((bf16[2,64,768]{2,0,1:T(2,128)(2,1)}), bf16[2,1024,768]{2,0,1:T(2,128)(2,1)}) %all-gather.10.cloned.1.call-update) | async-done | bytes 3145744 | tf_op jit(solution)/shard_map/all_gather | solution.py:90
  167.8 7.0 copy.135
  174.8 2.0 copy.138
  176.8 16.0 %while.37 = (s32[]{:T(128)}, f32[2,2,6,64]{3,2,1,0:T(8,128)}, bf16[2,2,64,384]{3,2,0,1:T(8,128)(2,1)}, bf16[2,2,64,384]{3,2,1,0:T(8,128)(2,1)}, bf16[2,2,1024,38...) while((s32[]{:T(128)}, f32[2,2,6,64]{3,2,1,0:T(8,128)}, ...), condition=%wide.region_3.4_spmd.clone, body=%wide.region_0.3_spmd.clone.sunk | while | flops 209978624 | bytes 21468332 | solution.py:111
  177.6 2.2 constant_dynamic-slice_fusion.23
  185.6 2.2 constant_dynamic-slice_fusion.23
  193.8 43.9 %all-gather.12.cloned.1.call-done = bf16[1536,768]{1,0:T(8,128)(2,1)} async-done(((bf16[96,768]{1,0:T(8,128)(2,1)}), bf16[1536,768]{1,0:T(8,128)(2,1)}) %all-gather.12.cloned.1.call-update) | async-done | bytes 2359312 | tf_op jit(solution)/shard_map/all_gather | solution.py:87
  237.7 2.6 broadcast_select_fusion
  240.3 2.2 collective-permute-start.1
  242.5 7.3 collective-permute-start
  249.8 64.3 %all-gather = bf16[32,48,31]{1,2,0:T(8,128)(2,1)S(1)} all-gather(bf16[1,48,31]{1,2,0:T(8,128)(2,1)S(1)} %bitcast.210), channel_id=1, replica_groups=mesh['dp'=32,'ctx'=16] {'dp'}, dimensions={0}, use_global_device_ids=true | all-gather | bytes 98208 | tf_op jit(solution)/shard_map/all_gather | solution.py:85
  314.8 2.7 fusion.54
  318.7 1.9 fusion.49
  320.5 1.9 fusion.43
  323.2 11.0 collective-permute-start.3
  334.2 6.8 collective-permute-start.2
  342.9 2.3 fusion.52
  345.5 2.2 bitcast_convert_fusion
  348.8 45.4 %all-gather.18.cloned.1.call-done = bf16[16,31,1536]{2,1,0:T(8,128)(2,1)} async-done(((bf16[1,31,1536]{2,1,0:T(8,128)(2,1)}), bf16[16,31,1536]{2,1,0:T(8,128)(2,1)}) %all-gather.18.cloned.1.call-update) | async-done | bytes 1523728 | tf_op jit(solution)/shard_map/all_gather | solution.py:12
  397.0 95.0 %reduce-scatter.6.cloned.1.call-done = bf16[96,768]{1,0:T(8,128)(2,1)} async-done(((bf16[1536,768]{1,0:T(8,128)(2,1)}), bf16[96,768]{1,0:T(8,128)(2,1)}) %reduce-scatter.6.cloned.1.call-update) | async-done | bytes 147472 | tf_op jit(solution)/shard_map/reduce_scatter | solution.py:252
  499.3 42.4 %all_gather.37 = f32[2,1024,12]{2,0,1:T(2,128)S(1)} all-gather(f32[2,64,12]{2,0,1:T(2,128)S(1)} %copy.162), channel_id=1, replica_groups=mesh['dp'=32,'ctx'=16] {'ctx'}, dimensions={1}, use_global_device_ids=true | all-gather | bytes 104448 | tf_op jit(solution)/shard_map/all_gather | solution.py:184
  542.8 28.9 %all-gather.14.cloned.1.call-done = bf16[2,1024,768]{2,0,1:T(2,128)(2,1)} async-done(((bf16[2,64,768]{2,0,1:T(2,128)(2,1)}), bf16[2,1024,768]{2,0,1:T(2,128)(2,1)}) %all-gather.14.cloned.1.call-update) | async-done | bytes 3145744 | tf_op jit(solution)/shard_map/all_gather | solution.py:192
  571.7 8.7 copy.160
  584.0 29.7 %while.38 = (s32[]{:T(128)}, f32[2,2,64,384]{2,3,1,0:T(8,128)}, bf16[2,2,1024,384]{2,3,1,0:T(8,128)(2,1)}, bf16[2,2,64,384]{3,2,1,0:T(8,128)(2,1)}, f32[2,2,6,64...) while((s32[]{:T(128)}, f32[2,2,64,384]{2,3,1,0:T(8,128)}, ...), condition=%wide.region_6.7_spmd.clone, body=%wide.region_5.6_spmd.clone.sunk | while | flops 306710528 | bytes 19099784 | solution.py:170
  584.0 2.2 constant_dynamic-slice_fusion.25
  588.9 2.2 fusion.108
  594.7 3.4 fusion.109
  598.9 2.2 constant_dynamic-slice_fusion.25
  603.8 2.2 fusion.108
  609.6 3.4 fusion.109
  616.0 39.9 %all_gather.39 = f32[2,1024,12]{2,0,1:T(2,128)S(1)} all-gather(f32[2,64,12]{2,0,1:T(2,128)} %copy.165), channel_id=1, replica_groups=mesh['dp'=32,'ctx'=16] {'ctx'}, dimensions={1}, use_global_device_ids=true | all-gather | bytes 104448 | tf_op jit(solution)/shard_map/all_gather | solution.py:185
  656.3 57.5 %reduce-scatter.8.cloned.1.call-done = bf16[48,31]{1,0:T(8,128)(2,1)} async-done(((bf16[1536,31]{1,0:T(8,128)(2,1)}), bf16[48,31]{1,0:T(8,128)(2,1)}) %reduce-scatter.8.cloned.1.call-update) | async-done | bytes 2992
  715.2 288.5 %all-reduce.3.cloned.1.call-done = bf16[96,768]{1,0:T(8,128)(2,1)} async-done(((bf16[96,768]{1,0:T(8,128)(2,1)}), bf16[96,768]{1,0:T(8,128)(2,1)}) %all-reduce.3.cloned.1.call-update) | async-done | bytes 147472
  1005.3 91.6 %all-gather.16.cloned.1.call-done = bf16[2,1024,768]{2,1,0:T(8,128)(2,1)} async-done(((bf16[2,64,768]{2,1,0:T(8,128)(2,1)}), bf16[2,1024,768]{2,1,0:T(8,128)(2,1)}) %all-gather.16.cloned.1.call-update) | async-done | bytes 3145744 | tf_op jit(solution)/shard_map/all_gather | solution.py:193
  1097.0 5.8 reshape.201
  1102.8 6.8 copy.164
  1110.6 34.6 %while.39 = (s32[]{:T(128)}, f32[2,2,64,384]{2,3,1,0:T(8,128)}, bf16[2,2,64,384]{2,3,1,0:T(8,128)(2,1)}, bf16[2,2,1024,384]{2,3,0,1:T(8,128)(2,1)}, bf16[2,2,64,...) while((s32[]{:T(128)}, f32[2,2,64,384]{2,3,1,0:T(8,128)}, ...), condition=%wide.region_8.9_spmd.clone, body=%wide.region_7.8_spmd.clone.sunk | while | flops 410517632 | bytes 39764904 | solution.py:232
  1113.3 2.2 fusion.117
  1119.9 3.3 fusion.118
  1124.0 3.0 fusion.119
  1130.6 2.3 fusion.117
  1137.2 3.3 fusion.118
  1141.4 3.0 fusion.119
  (184 shorter events, 80.1 us)
Async XLA Ops:
  7.2 87.1 %all-gather.8.cloned.1.call-start = ((), (), s32[]{:S(2)}) async-start(), calls=%async_computation.2 | async-start | bytes 3342336 | tf_op jit(solution)/shard_map/all_gather | solution.py:89
  9.0 158.8 %all-gather.10.cloned.1.call-start = ((), (), s32[]{:S(2)}) async-start(), calls=%async_computation.3 | async-start | bytes 3342336 | tf_op jit(solution)/shard_map/all_gather | solution.py:90
  10.9 226.8 %all-gather.12.cloned.1.call-start = ((), (), s32[]{:S(2)}) async-start(), calls=%async_computation.4 | async-start | bytes 2506752 | tf_op jit(solution)/shard_map/all_gather | solution.py:87
  89.1 305.1 %all-gather.18.cloned.1.call-start = ((), (), s32[]{:S(2)}) async-start(), calls=%async_computation.8 | async-start | bytes 1671168 | tf_op jit(solution)/shard_map/all_gather | solution.py:12
  90.8 0.5 copy-start.16
  182.9 1.2 copy-start.12
  184.2 0.7 copy-start.13
  190.9 1.2 copy-start.12
  192.2 0.7 copy-start.13
  192.8 57.0 %copy-start.15 = (bf16[31,48]{1,0:T(8,128)(2,1)S(1)}, bf16[31,48]{1,0:T(8,128)(2,1)}, u32[]{:S(2)}) copy-start(bf16[31,48]{1,0:T(8,128)(2,1)} %param.19) | copy-start | bytes 8932
  240.3 74.3 %collective-permute-start.1 = (bf16[2,15,1536]{2,1,0:T(8,128)(2,1)S(1)}, bf16[2,15,1536]{2,1,0:T(8,128)(2,1)S(1)}, u32[]{:S(2)}, u32[]{:S(2)}) collective-permute-start(bf16[2,15,1536]{2,1,0:T(8,128)(2,1)S(1)} %get-tuple-element.409), channel_id=1, source_target_pairs={{1,0},{2,1},{3,2},{4,3},{5,4},{6,5},{7,6},{8,7},{9,8},{10,9},{11,1... | collective-permute-start | bytes 276488 | tf_op jit(solution)/shard_map/ppermute | solution.py:26
  242.5 72.1 %collective-permute-start = (bf16[2,15,1536]{2,1,0:T(8,128)(2,1)S(1)}, bf16[2,15,1536]{2,1,0:T(8,128)(2,1)S(1)}, u32[]{:S(2)}, u32[]{:S(2)}) collective-permute-start(bf16[2,15,1536]{2,1,0:T(8,128)(2,1)S(1)} %get-tuple-element.408), channel_id=1, source_target_pairs={{0,1},{1,2},{2,3},{3,4},{4,5},{5,6},{6,7},{7,8},{8,9},{9,10},{10,1... | collective-permute-start | bytes 276488 | tf_op jit(solution)/shard_map/ppermute | solution.py:25
  314.8 2.7 copy-start.4
  323.2 168.8 %reduce-scatter.6.cloned.1.call-start = ((), (), s32[]{:S(2)}) async-start(), calls=%async_computation.7 | async-start | bytes 2506752 | tf_op jit(solution)/shard_map/reduce_scatter | solution.py:252
  323.2 18.2 %collective-permute-start.3 = (bf16[2,15,1536]{2,1,0:T(8,128)(2,1)S(1)}, bf16[2,15,1536]{2,1,0:T(8,128)(2,1)S(1)}, u32[]{:S(2)}, u32[]{:S(2)}) collective-permute-start(bf16[2,15,1536]{2,1,0:T(8,128)(2,1)S(1)} %get-tuple-element.407), channel_id=1, source_target_pairs={{1,0},{2,1},{3,2},{4,3},{5,4},{6,5},{7,6},{8,7},{9,8},{10,9},{11,1... | collective-permute-start | bytes 276488 | tf_op jit(solution)/shard_map/ppermute | solution.py:26
  334.2 8.5 collective-permute-start.2
  345.2 2.6 copy-start.9
  345.5 146.7 %copy-start.2 = (bf16[2,64,1536]{2,1,0:T(8,128)(2,1)}, bf16[2,64,1536]{2,1,0:T(8,128)(2,1)S(1)}, u32[]{:S(2)}) copy-start(bf16[2,64,1536]{2,1,0:T(8,128)(2,1)S(1)} %fusion.48) | copy-start | bytes 1179652
  347.8 144.5 %copy-start.1 = (bf16[1536,768]{1,0:T(8,128)(2,1)S(1)}, bf16[1536,768]{1,0:T(8,128)(2,1)}, u32[]{:S(2)}) copy-start(bf16[1536,768]{1,0:T(8,128)(2,1)} %all-gather.12.cloned.1.call-done) | copy-start | bytes 7077892
  347.8 145.7 %copy-start.10 = (bf16[2,64,768]{2,1,0:T(8,128)(2,1)S(1)}, bf16[2,64,768]{2,1,0:T(8,128)(2,1)}, u32[]{:S(2)}) copy-start(bf16[2,64,768]{2,1,0:T(8,128)(2,1)} %param.16) | copy-start | bytes 589828
  347.8 223.9 %all-gather.14.cloned.1.call-start = ((), (), s32[]{:S(2)}) async-start(), calls=%async_computation.5 | async-start | bytes 3342336 | tf_op jit(solution)/shard_map/all_gather | solution.py:192
  348.8 144.7 %copy-start.11 = (bf16[2,64,768]{2,1,0:T(8,128)(2,1)S(1)}, bf16[2,64,768]{2,1,0:T(8,128)(2,1)}, u32[]{:S(2)}) copy-start(bf16[2,64,768]{2,1,0:T(8,128)(2,1)} %param.17) | copy-start | bytes 589828
  348.8 365.1 %reduce-scatter.8.cloned.1.call-start = ((), (), s32[]{:S(2)}) async-start(), calls=%async_computation.9 | async-start | bytes 405504
  395.9 101.7 %copy-start.14 = (bf16[2,2,64,384]{3,2,0,1:T(8,128)(2,1)S(1)}, bf16[2,2,64,384]{3,2,0,1:T(8,128)(2,1)}, u32[]{:S(2)}) copy-start(bf16[2,2,64,384]{3,2,0,1:T(8,128)(2,1)} %get-tuple-element.145) | copy-start | bytes 589828
  396.9 606.9 %all-reduce.3.cloned.1.call-start = ((), (), s32[]{:S(2)}) async-start(), calls=%async_computation.10 | async-start | bytes 294912
  492.0 604.9 %all-gather.16.cloned.1.call-start = ((), (), s32[]{:S(2)}) async-start(), calls=%async_computation.6 | async-start | bytes 3342336 | tf_op jit(solution)/shard_map/all_gather | solution.py:193
  542.8 37.6 %copy-start.3 = (bf16[2,64,768]{2,1,0:T(8,128)(2,1)S(1)}, bf16[2,64,768]{2,1,0:T(8,128)(2,1)}, u32[]{:S(2)}) copy-start(bf16[2,64,768]{2,1,0:T(8,128)(2,1)} %fusion.44) | copy-start | bytes 589828
  1102.8 7.8 copy-start.17
  1110.6 5.6 copy-start.7
  1113.3 2.8 copy-start
  1124.0 3.0 copy-start.5
  1124.0 3.8 copy-start.8
  1127.1 0.8 copy-start.6
  1127.9 5.6 copy-start.7
  1130.6 2.8 copy-start
  1141.4 3.0 copy-start.5
  1141.4 3.8 copy-start.8
  1144.4 0.8 copy-start.6
Sparse Core Ops, SparseCore 0:
  11.8 82.3 all-gather.7
  98.1 69.6 all-gather.9
  171.7 65.9 all-gather.11
  323.3 70.9 all-gather.17
  398.9 93.0 reduce-scatter.5
  495.7 76.0 all-gather.13
  574.5 139.2 reduce-scatter.7
  717.0 286.7 all-reduce.2
  1007.1 89.7 all-gather.15
